TPU v7x, 256 devices: a whole 4x4x8 slice. The times are simulated.
256 devices in a mesh: dom: 16 (over y, x), feat: 16 (over z, core).
Axes of the slice: x: 4, y: 4, z: 8, core: 2. Of those that a mesh axis runs over, the one named last changes fastest.
Arguments:
- feature_table: float32 [1024, 131072], P('feat', 'dom'), may hold values from -6 to 6
- seed_ids: int32 [16384], P('dom'), may hold values from 0 to 8191
- neighbours: int32 [15, 16384], P(None, 'dom'), may hold values from 0 to 8191
- owners: int32 [1024, 1], P('dom'), may hold values from 0 to 15; in each aligned block of 64 rows (0 to 63, 64 to 127, ...) at most 8 rows name the same one
- blocks: int32 [1024], P('dom'), may hold values from 0 to 63
- counts: int32 [1024], P('dom'), may hold values from 1 to 128
- w_self: float32 [1024, 1024], P('feat'), may hold values from -0.1875 to 0.1875
- w_neigh: float32 [1024, 1024], P('feat'), may hold values from -0.5 to 0.5
- out_bias: float32 [1024], replicated, may hold values from -3 to 3
- cotangent: bfloat16 [16384, 1024], P(('dom', 'feat')), may hold values from -0.046875 to 0.046875
Outputs:
- hidden: bfloat16 [16384, 1024], P(('dom', 'feat'))
- grad_self: float32 [1024, 1024], P('feat')
- grad_neigh: float32 [1024, 1024], P('feat')
Inputs may be any that keep to these rules, and one draw needn't show every extreme that they name: `owners`: among the 64 frontier entries of one partition no owner appears more than 8 times.
All inputs are finite; a program needn't handle non-finite values.
Results may differ from a plain program's by a relative error of at most 0.003.
Values may be sent and summed in bfloat16 or wider, within the bound.
No kernel may reach another device: no remote copies, remote signals or barrier semaphores. Data moves between devices by JAX's collectives and lax.ppermute only.
A program may use at most 128 MiB of HBM per device.

v0:
```python
import jax
import jax.numpy as jnp
from jax import lax
from jax.sharding import PartitionSpec as P

FAN = 15
BLOCK = 128
SLOTS = 8


def silu_slope(preact):
    sigma = jax.nn.sigmoid(preact)
    return sigma * (1.0 + preact * (1.0 - sigma))


def contract(left, right):
    return lax.dot_general(
        left,
        right,
        (((0,), (0,)), ((), ())),
        precision=lax.Precision.HIGHEST,
        preferred_element_type=jnp.float32,
    )


def product(left, right):
    return lax.dot_general(
        left,
        right,
        (((1,), (0,)), ((), ())),
        precision=lax.Precision.HIGHEST,
        preferred_element_type=jnp.float32,
    )


def body(
    feature_table,
    seed_ids,
    neighbours,
    owners,
    blocks,
    counts,
    w_self,
    w_neigh,
    out_bias,
    cotangent,
):
    cols_dev = feature_table.shape[0]
    node_rows = feature_table.shape[1]
    n_dom = lax.axis_size("dom")
    front = owners.shape[0]
    seeds_dev = seed_ids.shape[0]
    fanout = neighbours.shape[0]
    owner_ids = owners[:, 0]
    one_hot = (owner_ids[:, None] == jnp.arange(n_dom, dtype=jnp.int32)[None, :]).astype(jnp.int32)
    slot_rank = jnp.sum(jnp.cumsum(one_hot, axis=0) * one_hot, axis=1) - 1
    outgoing_ids = jnp.zeros((n_dom, SLOTS), jnp.int32).at[owner_ids, slot_rank].set(blocks)
    requested = lax.all_to_all(outgoing_ids, "dom", split_axis=0, concat_axis=0, tiled=True)
    table_rows = jnp.transpose(feature_table)
    block_rows = table_rows.reshape(node_rows // BLOCK, BLOCK, cols_dev)
    outgoing = block_rows[requested.reshape(-1)].reshape(n_dom, SLOTS, BLOCK, cols_dev)
    arrived = lax.all_to_all(outgoing, "dom", split_axis=0, concat_axis=0, tiled=True)
    arrived_flat = arrived.reshape(n_dom * SLOTS, BLOCK, cols_dev)
    frontier = arrived_flat[owner_ids * SLOTS + slot_rank]
    row_valid = jnp.arange(BLOCK, dtype=jnp.int32)[None, :] < counts[:, None]
    frontier = jnp.where(row_valid[:, :, None], frontier, 0.0).reshape(front * BLOCK, cols_dev)
    picked = frontier[neighbours.reshape(-1)].reshape(fanout, seeds_dev, cols_dev)
    neighbour_mean = jnp.sum(picked, axis=0) * (1.0 / FAN)
    self_rows = table_rows[seed_ids]
    stacked = jnp.concatenate([self_rows, neighbour_mean], axis=1)
    weight_cat = jnp.concatenate([w_self, w_neigh], axis=0)
    preact = (
        lax.psum_scatter(product(stacked, weight_cat), "feat", scatter_dimension=0, tiled=True)
        + out_bias[None, :]
    )
    hidden = jax.nn.silu(preact).astype(jnp.bfloat16)
    slope = (cotangent.astype(jnp.float32) * silu_slope(preact)).astype(jnp.bfloat16)
    grad_local = contract(
        stacked, lax.all_gather(slope, "feat", axis=0, tiled=True).astype(jnp.float32)
    )
    grad_total = lax.psum(grad_local, "dom")
    return (hidden, grad_total[:cols_dev], grad_total[cols_dev:])


def solution(mesh):
    return jax.shard_map(
        body,
        mesh=mesh,
        in_specs=(
            P("feat", "dom"),
            P("dom"),
            P(None, "dom"),
            P("dom", None),
            P("dom"),
            P("dom"),
            P("feat", None),
            P("feat", None),
            P(),
            P(("dom", "feat"), None),
        ),
        out_specs=(P(("dom", "feat"), None), P("feat", None), P("feat", None)),
        check_vma=False,
    )
```

profile of v0, /device:TPU:32, one launch (start us, length us, event | category | flops | bytes accessed | tf_op | source)
XLA Modules:
  0.0 396.3 jit_solution(11303320467679522365)
XLA Ops:
  7.2 0.7 fusion.5
  7.9 0.1 reduce_window_sum.11
  8.0 0.8 select_reduce_fusion
  8.8 0.7 fusion.10
  9.5 5.7 %scatter_fusion = s32[16,8]{0,1:T(8,128)S(1)} fusion(s32[16,8]{0,1:T(8,128)S(1)} %broadcast_in_dim.18, s32[64]{0:T(128)S(1)} %get-tuple-element.8, s32[64]{0:T(128)} %param.14), kind=kCustom, calls=%fused_computation.4 | custom fusion | bytes 1280 | tf_op jit(solution)/shard_map/scatter | solution.py:57
  15.3 0.7 copy.24
  15.9 7.0 %all-to-all-start = ((s32[16,1,8]{2,1,0:T(1,128)}), s32[16,1,8]{2,1,0:T(1,128)S(1)}, u32[]{:S(2)}, u32[]{:S(2)}) async-start(s32[16,1,8]{2,1,0:T(1,128)} %copy.24), calls=%async_computation | async-start | bytes 16384 | tf_op jit(solution)/shard_map/all_to_all | solution.py:58
  23.0 0.7 fusion.6
  23.7 3.8 copy.23
  27.5 2.9 all-to-all-done
  30.4 0.5 broadcast.144
  31.0 0.7 reduce.3
  31.6 0.1 reshape.132
  31.7 6.5 %gather_fusion.1 = f32[128,128,64]{2,1,0:T(8,128)} fusion(f32[64,128,64]{2,1,0:T(8,128)} %bitcast.37, s32[1024]{0:T(1024)S(1)} %pad_clamp_fusion.1), kind=kCustom, calls=%fused_computation.1 | custom fusion | bytes 8389120 | tf_op jit(solution)/shard_map/gather | solution.py:61
  38.2 6.8 %copy.25 = f32[128,128,64]{1,2,0:T(8,128)} copy(f32[128,128,64]{2,1,0:T(8,128)} %gather_fusion.1) | data formatting | bytes 8388608 | tf_op jit(solution)/shard_map/gather | solution.py:61
  45.0 0.0 copy-start.5
  45.0 0.0 copy-start.3
  45.1 4.7 %all-to-all-start.1 = ((f32[16,8,128,64]{2,3,1,0:T(8,128)}), f32[16,8,128,64]{2,3,1,0:T(8,128)}, u32[]{:S(2)}, u32[]{:S(2)}) async-start(f32[16,8,128,64]{2,3,1,0:T(8,128)} %bitcast.40), calls=%async_computation.1 | async-start | bytes 8388608 | tf_op jit(solution)/shard_map/all_to_all | solution.py:62
  49.7 0.0 reduce-scatter.2.cloned.1.call-start
  49.8 0.0 copy-done.5
  49.8 0.0 copy-done.3
  49.8 0.1 copy.30
  49.9 5.0 %gather_fusion = f32[1024,64]{1,0:T(8,128)S(1)} fusion(f32[8192,64]{1,0:T(8,128)} %bitcast.38, s32[1024]{0:T(1024)S(1)} %fusion.7), kind=kCustom, calls=%fused_computation | custom fusion | bytes 528384 | tf_op jit(solution)/shard_map/gather | solution.py:69
  54.9 0.1 compare_select_fusion
  55.0 55.8 %all-to-all-done.1 = f32[16,8,128,64]{2,3,1,0:T(8,128)} async-done(((f32[16,8,128,64]{2,3,1,0:T(8,128)}), f32[16,8,128,64]{2,3,1,0:T(8,128)}, u32[]{:S(2)}, u32[]{:S(2)}) %all-to-all-start.1) | async-done | bytes 4194336 | tf_op jit(solution)/shard_map/all_to_all | solution.py:62
  110.8 2.9 gather_fusion.2
  113.7 2.7 copy.28
  116.4 7.4 %bitcast_select_fusion = f32[8192,64]{1,0:T(8,128)} fusion(f32[64,128,64]{2,1,0:T(8,128)} %copy.28, pred[8192]{0:T(1024)(128)(4,1)S(1)} %fusion.6), kind=kLoop, calls=%fused_computation.5 | loop fusion | flops 524288 | bytes 4202496 | tf_op jit(solution)/shard_map/jit(_where)/select_n | solution.py:66
  123.8 53.7 %gather_fusion.3 = f32[15360,64]{1,0:T(8,128)} fusion(f32[8192,64]{1,0:T(8,128)} %bitcast_select_fusion, s32[15360]{0:T(1024)S(1)} %broadcast_clamp_fusion), kind=kCustom, calls=%fused_computation.3 | custom fusion | bytes 7925760 | tf_op jit(solution)/shard_map/gather | solution.py:67
  177.5 3.9 reduce_sum.19
  181.4 0.0 copy-done
  181.4 0.0 copy-done.1
  181.4 0.0 copy-start.2
  181.4 0.0 copy-start.4
  181.5 5.1 %fusion = f32[1024,1024]{1,0:T(8,128)} fusion(f32[64,1024]{1,0:T(8,128)S(1)} %copy-done, f32[64,1024]{1,0:T(8,128)S(1)} %copy-done.1, f32[1024,64]{1,0:T(8,128)S(1)} %broadcast_multiply_fusion, f32[1024,64]{1,0:T(8,128)S(1)} %gather_fusion), kind=kOutput, calls=%fused_computation.7 | convolution fusion | flops 1610874880 | bytes 5242880 | tf_op jit(solution)/shard_map/dot_general | solution.py:27
  186.5 0.0 reduce-scatter.2.cloned.1.call-update
  186.5 0.0 all-gather.2.cloned.1.call-start
  186.6 59.8 %reduce-scatter.2.cloned.1.call-done = f32[64,1024]{1,0:T(8,128)} async-done(((f32[1024,1024]{1,0:T(8,128)}), f32[64,1024]{1,0:T(8,128)}) %reduce-scatter.2.cloned.1.call-update) | async-done | bytes 262160 | tf_op jit(solution)/shard_map/reduce_scatter | solution.py:73
  246.4 0.0 copy-done.2
  246.4 0.0 copy-done.4
  246.4 1.8 multiply_convert_fusion
  248.2 0.0 all-gather.2.cloned.1.call-update
  248.2 0.0 all-reduce.2.cloned.1.call-start
  248.3 41.5 %all-gather.2.cloned.1.call-done = bf16[1024,1024]{1,0:T(8,128)(2,1)} async-done(((bf16[64,1024]{1,0:T(8,128)(2,1)}), bf16[1024,1024]{1,0:T(8,128)(2,1)}) %all-gather.2.cloned.1.call-update) | async-done | bytes 2097168 | tf_op jit(solution)/shard_map/all_gather | solution.py:79
  289.8 3.7 fusion.4
  293.4 0.0 all-reduce.2.cloned.1.call-update
  293.4 94.4 %all-reduce.2.cloned.1.call-done = f32[128,1024]{1,0:T(8,128)} async-done(((f32[128,1024]{1,0:T(8,128)}), f32[128,1024]{1,0:T(8,128)}) %all-reduce.2.cloned.1.call-update) | async-done | bytes 524304 | tf_op jit(solution)/shard_map/psum | solution.py:81
  387.9 1.9 fusion.14
  (9 shorter events, 0.1 us)
Async XLA Ops:
  15.9 14.5 %all-to-all-start = ((s32[16,1,8]{2,1,0:T(1,128)}), s32[16,1,8]{2,1,0:T(1,128)S(1)}, u32[]{:S(2)}, u32[]{:S(2)}) async-start(s32[16,1,8]{2,1,0:T(1,128)} %copy.24), calls=%async_computation | async-start | bytes 16384 | tf_op jit(solution)/shard_map/all_to_all | solution.py:58
  45.0 4.7 %copy-start.5 = (s32[1024]{0:T(1024)S(1)}, s32[1024]{0:T(1024)}, u32[]{:S(2)}) copy-start(s32[1024]{0:T(1024)} %param.11) | copy-start | bytes 12292
  45.0 4.7 %copy-start.3 = (s32[15,1024]{1,0:T(8,128)S(1)}, s32[15,1024]{1,0:T(8,128)}, u32[]{:S(2)}) copy-start(s32[15,1024]{1,0:T(8,128)} %param.12) | copy-start | bytes 184324
  45.1 65.7 %all-to-all-start.1 = ((f32[16,8,128,64]{2,3,1,0:T(8,128)}), f32[16,8,128,64]{2,3,1,0:T(8,128)}, u32[]{:S(2)}, u32[]{:S(2)}) async-start(f32[16,8,128,64]{2,3,1,0:T(8,128)} %bitcast.40), calls=%async_computation.1 | async-start | bytes 8388608 | tf_op jit(solution)/shard_map/all_to_all | solution.py:62
  49.7 196.7 %reduce-scatter.2.cloned.1.call-start = ((), (), s32[]{:S(2)}) async-start(), calls=%async_computation.3 | async-start | bytes 4456448 | tf_op jit(solution)/shard_map/reduce_scatter | solution.py:73
  177.5 4.0 copy-start
  177.5 4.0 %copy-start.1 = (f32[64,1024]{1,0:T(8,128)S(1)}, f32[64,1024]{1,0:T(8,128)}, u32[]{:S(2)}) copy-start(f32[64,1024]{1,0:T(8,128)} %param.16) | copy-start | bytes 786436
  181.4 65.0 %copy-start.2 = (bf16[64,1024]{1,0:T(8,128)(2,1)S(1)}, bf16[64,1024]{1,0:T(8,128)(2,1)}, u32[]{:S(2)}) copy-start(bf16[64,1024]{1,0:T(8,128)(2,1)} %param.19) | copy-start | bytes 393220
  181.4 65.0 %copy-start.4 = (f32[1024]{0:T(1024)S(1)}, f32[1024]{0:T(1024)}, u32[]{:S(2)}) copy-start(f32[1024]{0:T(1024)} %param.18) | copy-start | bytes 12292
  186.5 103.2 %all-gather.2.cloned.1.call-start = ((), (), s32[]{:S(2)}) async-start(), calls=%async_computation.4 | async-start | bytes 2228224 | tf_op jit(solution)/shard_map/all_gather | solution.py:79
  248.2 139.7 %all-reduce.2.cloned.1.call-start = ((), (), s32[]{:S(2)}) async-start(), calls=%async_computation.5 | async-start | bytes 1048576 | tf_op jit(solution)/shard_map/psum | solution.py:81
Sparse Core Ops, SparseCore 0:
  186.6 59.7 reduce-scatter.1
  248.8 40.9 all-gather.1
  293.6 94.2 all-reduce.1
where the time goes:
time: 397 us; the launch traced here: 396 us
  waiting for transfers between devices  255 us (64%)
  local copies, waits for them, and re-layouts  90.3 us (23%)
  other arithmetic  17 us (4%)
  between operations  13.9 us (4%)
  starting transfers between devices  11.8 us (3%)
  matrix products  8.71 us (2%)
    psum x1, waiting for transfers between devices, body(): grad_total = lax.psum(grad_local, 'dom')  94.4 us
    reduce_scatter x1, waiting for transfers between devices, body(): lax.psum_scatter(product(stacked, weight_cat), 'feat', scatter_dimension=...  59.8 us
    all_to_all x1, waiting for transfers between devices, body(): lax.all_to_all(outgoing, 'dom', split_axis=0, concat_axis=0, tiled=True)  55.8 us
    gather x1, local copies, waits for them, and re-layouts, body(): frontier[neighbours.reshape(-1)].reshape(fanout, seeds_dev, cols_dev)  53.7 us
    all_gather x1, waiting for transfers between devices, body(): lax.all_gather(slope, 'feat', axis=0, tiled=True).astype(jnp.float32)  41.5 us
    gather x2, local copies, waits for them, and re-layouts, body(): block_rows[requested.reshape(-1)].reshape(n_dom, SLOTS, BLOCK, cols_dev)  13.3 us
  transfers between devices with their start and end apart: 5, of which 5 were waited for; matrix products, arithmetic and copies ran while one was open for 2% of the time, Pallas kernels for 0%

commit v1 on v0

--- a/solution.py
+++ b/solution.py
@@ -76,7 +76,10 @@
     hidden = jax.nn.silu(preact).astype(jnp.bfloat16)
     slope = (cotangent.astype(jnp.float32) * silu_slope(preact)).astype(jnp.bfloat16)
     grad_local = contract(
-        stacked, lax.all_gather(slope, "feat", axis=0, tiled=True).astype(jnp.float32)
+        stacked,
+        jnp.concatenate(
+            lax.all_to_all(jnp.stack([slope] * lax.axis_size("feat")), "feat", 0, 0), axis=0
+        ).astype(jnp.float32),
     )
     grad_total = lax.psum(grad_local, "dom")
     return (hidden, grad_total[:cols_dev], grad_total[cols_dev:])

time: 397 us -> 411 us (1.035)
  blocking collectives: 0 us -> 55.8 us
  waiting for transfers between devices: 255 us -> 214 us
    all_to_all x0 -> x1, blocking collectives: none -> 55.8 us  [body(): lax.all_to_all(jnp.stack([slope] * lax.axis_size('feat')), 'feat', 0, 0)]
    all_gather x1 -> x0, waiting for transfers between devices: 41.5 us -> none  [body(): lax.all_gather(slope, 'feat', axis=0, tiled=True).astype(jnp.float32)]
  transfers between devices with their start and end apart: 5 -> 4, of which waited for: 5 -> 4; matrix products, arithmetic and copies ran while one was open for 2% -> 2% of each run, Pallas kernels for 0% -> 0%
where the time goes in v1:
time: 411 us; the launch traced here: 410 us
  waiting for transfers between devices  214 us (52%)
  local copies, waits for them, and re-layouts  90.2 us (22%)
  blocking collectives  55.8 us (14%)
  other arithmetic  16.9 us (4%)
  between operations  14.2 us (3%)
  starting transfers between devices  11.8 us (3%)
  matrix products  7.16 us (2%)
    psum x1, waiting for transfers between devices, body(): grad_total = lax.psum(grad_local, 'dom')  95 us
    reduce_scatter x1, waiting for transfers between devices, body(): lax.psum_scatter(product(stacked, weight_cat), 'feat', scatter_dimension=...  60 us
    all_to_all x1, waiting for transfers between devices, body(): lax.all_to_all(outgoing, 'dom', split_axis=0, concat_axis=0, tiled=True)  55.8 us
    all_to_all x1, blocking collectives, body(): lax.all_to_all(jnp.stack([slope] * lax.axis_size('feat')), 'feat', 0, 0)  55.8 us
    gather x1, local copies, waits for them, and re-layouts, body(): frontier[neighbours.reshape(-1)].reshape(fanout, seeds_dev, cols_dev)  53.3 us
    gather x2, local copies, waits for them, and re-layouts, body(): block_rows[requested.reshape(-1)].reshape(n_dom, SLOTS, BLOCK, cols_dev)  13.3 us
  transfers between devices with their start and end apart: 4, of which 4 were waited for; matrix products, arithmetic and copies ran while one was open for 2% of the time, Pallas kernels for 0%

profile of v1, /device:TPU:32, one launch (start us, length us, event | category | flops | bytes accessed | tf_op | source)
XLA Modules:
  0.0 409.8 jit_solution(4215387338329041037)
XLA Ops:
  7.2 0.7 fusion.5
  7.9 0.1 reduce_window_sum.11
  8.0 0.8 select_reduce_fusion
  8.8 0.7 fusion.10
  9.5 5.7 %scatter_fusion = s32[16,8]{0,1:T(8,128)S(1)} fusion(s32[16,8]{0,1:T(8,128)S(1)} %broadcast_in_dim.18, s32[64]{0:T(128)S(1)} %get-tuple-element.8, s32[64]{0:T(128)} %param.14), kind=kCustom, calls=%fused_computation.4 | custom fusion | bytes 1280 | tf_op jit(solution)/shard_map/scatter | solution.py:57
  15.3 0.7 copy.24
  15.9 7.0 %all-to-all-start = ((s32[16,1,8]{2,1,0:T(1,128)}), s32[16,1,8]{2,1,0:T(1,128)S(1)}, u32[]{:S(2)}, u32[]{:S(2)}) async-start(s32[16,1,8]{2,1,0:T(1,128)} %copy.24), calls=%async_computation | async-start | bytes 16384 | tf_op jit(solution)/shard_map/all_to_all | solution.py:58
  23.0 0.7 fusion.6
  23.7 3.8 copy.23
  27.5 2.9 all-to-all-done
  30.4 0.5 broadcast.146
  31.0 0.7 reduce.3
  31.6 0.1 reshape.137
  31.7 6.5 %gather_fusion.1 = f32[128,128,64]{2,1,0:T(8,128)} fusion(f32[64,128,64]{2,1,0:T(8,128)} %bitcast.38, s32[1024]{0:T(1024)S(1)} %pad_clamp_fusion.1), kind=kCustom, calls=%fused_computation.1 | custom fusion | bytes 8389120 | tf_op jit(solution)/shard_map/gather | solution.py:61
  38.2 6.8 %copy.25 = f32[128,128,64]{1,2,0:T(8,128)} copy(f32[128,128,64]{2,1,0:T(8,128)} %gather_fusion.1) | data formatting | bytes 8388608 | tf_op jit(solution)/shard_map/gather | solution.py:61
  45.1 0.0 copy-start.5
  45.1 0.0 copy-start.3
  45.1 4.7 %all-to-all-start.1 = ((f32[16,8,128,64]{2,3,1,0:T(8,128)}), f32[16,8,128,64]{2,3,1,0:T(8,128)}, u32[]{:S(2)}, u32[]{:S(2)}) async-start(f32[16,8,128,64]{2,3,1,0:T(8,128)} %bitcast.41), calls=%async_computation.1 | async-start | bytes 8388608 | tf_op jit(solution)/shard_map/all_to_all | solution.py:62
  49.7 0.0 reduce-scatter.2.cloned.1.call-start
  49.8 0.0 copy-done.5
  49.8 0.0 copy-done.3
  49.8 0.1 copy.30
  49.9 5.0 %gather_fusion = f32[1024,64]{1,0:T(8,128)S(1)} fusion(f32[8192,64]{1,0:T(8,128)} %bitcast.39, s32[1024]{0:T(1024)S(1)} %fusion.7), kind=kCustom, calls=%fused_computation | custom fusion | bytes 528384 | tf_op jit(solution)/shard_map/gather | solution.py:69
  54.9 0.1 compare_select_fusion
  55.0 55.8 %all-to-all-done.1 = f32[16,8,128,64]{2,3,1,0:T(8,128)} async-done(((f32[16,8,128,64]{2,3,1,0:T(8,128)}), f32[16,8,128,64]{2,3,1,0:T(8,128)}, u32[]{:S(2)}, u32[]{:S(2)}) %all-to-all-start.1) | async-done | bytes 4194336 | tf_op jit(solution)/shard_map/all_to_all | solution.py:62
  110.8 2.9 gather_fusion.2
  113.7 2.7 copy.28
  116.4 7.4 %bitcast_select_fusion = f32[8192,64]{1,0:T(8,128)} fusion(f32[64,128,64]{2,1,0:T(8,128)} %copy.28, pred[8192]{0:T(1024)(128)(4,1)S(1)} %fusion.6), kind=kLoop, calls=%fused_computation.5 | loop fusion | flops 524288 | bytes 4202496 | tf_op jit(solution)/shard_map/jit(_where)/select_n | solution.py:66
  123.8 53.3 %gather_fusion.3 = f32[15360,64]{1,0:T(8,128)} fusion(f32[8192,64]{1,0:T(8,128)} %bitcast_select_fusion, s32[15360]{0:T(1024)S(1)} %broadcast_clamp_fusion), kind=kCustom, calls=%fused_computation.3 | custom fusion | bytes 7925760 | tf_op jit(solution)/shard_map/gather | solution.py:67
  177.1 0.0 copy-start
  177.1 3.9 reduce_sum.19
  181.1 0.0 copy-done
  181.1 0.0 copy-done.1
  181.1 0.0 copy-start.2
  181.1 0.0 copy-start.4
  181.1 5.1 %fusion = f32[1024,1024]{1,0:T(8,128)} fusion(f32[64,1024]{1,0:T(8,128)S(1)} %copy-done, f32[64,1024]{1,0:T(8,128)S(1)} %copy-done.1, f32[1024,64]{1,0:T(8,128)S(1)} %broadcast_multiply_fusion, f32[1024,64]{1,0:T(8,128)S(1)} %gather_fusion), kind=kOutput, calls=%fused_computation.7 | convolution fusion | flops 1610874880 | bytes 5242880 | tf_op jit(solution)/shard_map/dot_general | solution.py:27
  186.2 0.0 reduce-scatter.2.cloned.1.call-update
  186.2 0.0 all-reduce.2.cloned.1.call-start
  186.2 60.0 %reduce-scatter.2.cloned.1.call-done = f32[64,1024]{1,0:T(8,128)} async-done(((f32[1024,1024]{1,0:T(8,128)}), f32[64,1024]{1,0:T(8,128)}) %reduce-scatter.2.cloned.1.call-update) | async-done | bytes 262160 | tf_op jit(solution)/shard_map/reduce_scatter | solution.py:73
  246.3 0.0 copy-done.2
  246.3 0.0 copy-done.4
  246.3 1.7 multiply_convert_fusion
  248.0 0.3 stack.2
  248.2 55.8 %all_to_all.19 = bf16[16,64,1024]{2,1,0:T(8,128)(2,1)S(1)} all-to-all(bf16[16,64,1024]{2,1,0:T(8,128)(2,1)S(1)} %stack.2), channel_id=1, replica_groups=mesh['dom'=16,'feat'=16] {'feat'}, dimensions={0} | all-to-all | bytes 4194304 | tf_op jit(solution)/shard_map/all_to_all | solution.py:81
  304.0 2.1 fusion.4
  306.1 0.0 all-reduce.2.cloned.1.call-update
  306.1 95.0 %all-reduce.2.cloned.1.call-done = f32[128,1024]{1,0:T(8,128)} async-done(((f32[128,1024]{1,0:T(8,128)}), f32[128,1024]{1,0:T(8,128)}) %all-reduce.2.cloned.1.call-update) | async-done | bytes 524304 | tf_op jit(solution)/shard_map/psum | solution.py:84
  401.1 1.9 fusion.14
  (8 shorter events, 0.1 us)
Async XLA Ops:
  15.9 14.5 %all-to-all-start = ((s32[16,1,8]{2,1,0:T(1,128)}), s32[16,1,8]{2,1,0:T(1,128)S(1)}, u32[]{:S(2)}, u32[]{:S(2)}) async-start(s32[16,1,8]{2,1,0:T(1,128)} %copy.24), calls=%async_computation | async-start | bytes 16384 | tf_op jit(solution)/shard_map/all_to_all | solution.py:58
  45.1 4.7 %copy-start.5 = (s32[1024]{0:T(1024)S(1)}, s32[1024]{0:T(1024)}, u32[]{:S(2)}) copy-start(s32[1024]{0:T(1024)} %param.11) | copy-start | bytes 12292
  45.1 4.8 %copy-start.3 = (s32[15,1024]{1,0:T(8,128)S(1)}, s32[15,1024]{1,0:T(8,128)}, u32[]{:S(2)}) copy-start(s32[15,1024]{1,0:T(8,128)} %param.12) | copy-start | bytes 184324
  45.1 65.8 %all-to-all-start.1 = ((f32[16,8,128,64]{2,3,1,0:T(8,128)}), f32[16,8,128,64]{2,3,1,0:T(8,128)}, u32[]{:S(2)}, u32[]{:S(2)}) async-start(f32[16,8,128,64]{2,3,1,0:T(8,128)} %bitcast.41), calls=%async_computation.1 | async-start | bytes 8388608 | tf_op jit(solution)/shard_map/all_to_all | solution.py:62
  49.7 196.5 %reduce-scatter.2.cloned.1.call-start = ((), (), s32[]{:S(2)}) async-start(), calls=%async_computation.4 | async-start | bytes 4456448 | tf_op jit(solution)/shard_map/reduce_scatter | solution.py:73
  177.1 4.0 copy-start
  177.1 4.0 copy-start.1
  181.1 65.2 %copy-start.2 = (bf16[64,1024]{1,0:T(8,128)(2,1)S(1)}, bf16[64,1024]{1,0:T(8,128)(2,1)}, u32[]{:S(2)}) copy-start(bf16[64,1024]{1,0:T(8,128)(2,1)} %param.19) | copy-start | bytes 393220
  181.1 65.2 %copy-start.4 = (f32[1024]{0:T(1024)S(1)}, f32[1024]{0:T(1024)}, u32[]{:S(2)}) copy-start(f32[1024]{0:T(1024)} %param.18) | copy-start | bytes 12292
  186.2 214.9 %all-reduce.2.cloned.1.call-start = ((), (), s32[]{:S(2)}) async-start(), calls=%async_computation.5 | async-start | bytes 1048576 | tf_op jit(solution)/shard_map/psum | solution.py:84
Sparse Core Ops, SparseCore 0:
  186.3 59.9 reduce-scatter.1
  306.3 94.8 all-reduce.1
